TPU v7x, 256 devices: a whole 4x4x8 slice. The times are simulated.
256 devices in a mesh: bin: 4 (over x_lo, core), row: 64 (over z, x_hi, y).
Axes of the slice: x: 4 (x_hi: 2, x_lo: 2; x = x_hi * 2 + x_lo), y: 4, z: 8, core: 2. Of those that a mesh axis runs over, the one named last changes fastest.
Arguments:
- focusing: bfloat16 [12, 2, 4096, 4096], P('bin', None, 'row'), may hold values from -0.0625 to 0.0625
- snapshots: bfloat16 [12, 2, 4096, 128], P('bin', None, 'row'), may hold values from -6 to 6
Outputs:
- spectrum: float32 [2, 4096, 4096], P(None, 'row', 'bin')
All inputs are finite; a program needn't handle non-finite values.
Results may differ from a plain program's by a relative error of at most 0.0034.
Values may be sent and summed in bfloat16 or wider, within the bound.
A program may use at most 64 MiB of HBM per device.

v0:
```python
import jax
import jax.numpy as jnp
from jax import lax
from jax.sharding import PartitionSpec as P


def contract(left, right):
    return lax.dot_general(
        left, right, (((1,), (1,)), ((), ())), preferred_element_type=jnp.float32
    )


def on_device(focusing, snapshots):
    local_bins = focusing.shape[0]
    own_rows = focusing.shape[2]
    width = focusing.shape[3]
    count = snapshots.shape[3]
    scale = 1.0 / (local_bins * lax.axis_size("bin") * count)
    pieces = []
    for index in range(local_bins):
        matrix = focusing[index]
        piece = lax.all_gather(snapshots[index], "row", axis=1, tiled=True)
        new_real = jnp.dot(matrix[0], piece[0], preferred_element_type=jnp.float32) - jnp.dot(
            matrix[1], piece[1], preferred_element_type=jnp.float32
        )
        new_imag = jnp.dot(matrix[0], piece[1], preferred_element_type=jnp.float32) + jnp.dot(
            matrix[1], piece[0], preferred_element_type=jnp.float32
        )
        pieces.append(jnp.stack([new_real, new_imag]).astype(jnp.bfloat16))
    focused = jnp.stack(pieces)
    total = jnp.zeros((2, own_rows, width), jnp.float32)
    for index in range(local_bins):
        current = focused[index]
        gram_piece = lax.all_gather(current, "row", axis=1, tiled=True)
        real_part = contract(current[0], gram_piece[0]) + contract(current[1], gram_piece[1])
        imag_part = contract(current[1], gram_piece[0]) - contract(current[0], gram_piece[1])
        total = total + jnp.stack([real_part, imag_part])
    return lax.psum_scatter(total * scale, "bin", scatter_dimension=2, tiled=True)


def solution(mesh):
    placed = (P("bin", None, "row", None), P("bin", None, "row", None))
    return jax.shard_map(
        on_device, mesh=mesh, in_specs=placed, out_specs=P(None, "row", "bin"), check_vma=False
    )
```

profile of v0, /device:TPU:1, one launch (start us, length us, event | category | flops | bytes accessed | tf_op | source)
XLA Modules:
  0.0 767.7 jit_solution(13210433172321638339)
XLA Ops:
  6.5 1.6 fusion.50
  8.2 0.7 all-gather.20.cloned.1.call-update
  8.9 0.7 all-gather.16.cloned.1.call-update
  9.7 119.6 %all-gather.18.cloned.1.call-done = bf16[1,2,4096,128]{3,2,1,0:T(8,128)(2,1)} async-done(((bf16[1,2,64,128]{3,2,1,0:T(8,128)(2,1)}), bf16[1,2,4096,128]{3,2,1,0:T(8,128)(2,1)}) %all-gather.18.cloned.1.call-update) | async-done | bytes 2097168 | tf_op jit(solution)/shard_map/all_gather | solution.py:22
  129.2 1.7 fusion.18
  131.0 1.8 fusion.19
  132.8 1.5 fusion.10
  135.4 112.2 %all-gather.20.cloned.1.call-done = bf16[1,2,4096,128]{3,2,1,0:T(8,128)(2,1)} async-done(((bf16[1,2,64,128]{3,2,1,0:T(8,128)(2,1)}), bf16[1,2,4096,128]{3,2,1,0:T(8,128)(2,1)}) %all-gather.20.cloned.1.call-update) | async-done | bytes 2097168 | tf_op jit(solution)/shard_map/all_gather | solution.py:22
  247.5 1.7 fusion.22
  249.2 1.5 fusion.23
  252.1 113.7 %all-gather.16.cloned.1.call-done = bf16[1,2,4096,128]{3,2,1,0:T(8,128)(2,1)} async-done(((bf16[1,2,64,128]{3,2,1,0:T(8,128)(2,1)}), bf16[1,2,4096,128]{3,2,1,0:T(8,128)(2,1)}) %all-gather.16.cloned.1.call-update) | async-done | bytes 2097168 | tf_op jit(solution)/shard_map/all_gather | solution.py:22
  365.9 1.7 fusion.14
  367.5 1.5 fusion.15
  370.4 113.6 %all-gather.12.cloned.1.call-done = bf16[2,4096,128]{2,1,0:T(8,128)(2,1)} async-done(((bf16[2,64,128]{2,1,0:T(8,128)(2,1)}), bf16[2,4096,128]{2,1,0:T(8,128)(2,1)}) %all-gather.12.cloned.1.call-update) | async-done | bytes 2097168 | tf_op jit(solution)/shard_map/all_gather | solution.py:34
  484.0 2.8 fusion.21
  486.8 1.5 fusion.20
  488.3 113.9 %all-gather.14.cloned.1.call-done = bf16[2,4096,128]{2,1,0:T(8,128)(2,1)} async-done(((bf16[2,64,128]{2,1,0:T(8,128)(2,1)}), bf16[2,4096,128]{2,1,0:T(8,128)(2,1)}) %all-gather.14.cloned.1.call-update) | async-done | bytes 2097168 | tf_op jit(solution)/shard_map/all_gather | solution.py:34
  602.2 2.8 fusion.25
  605.5 114.8 %all-gather.10.cloned.1.call-done = bf16[2,4096,128]{2,1,0:T(8,128)(2,1)} async-done(((bf16[2,64,128]{2,1,0:T(8,128)(2,1)}), bf16[2,4096,128]{2,1,0:T(8,128)(2,1)}) %all-gather.10.cloned.1.call-update) | async-done | bytes 2097168 | tf_op jit(solution)/shard_map/all_gather | solution.py:34
  720.3 1.8 fusion.17
  723.2 0.7 copy-done.4
  724.4 1.1 copy-done.2
  727.7 1.7 fusion.7
  729.5 31.4 %reduce-scatter.2.cloned.1.call-done = f32[2,64,1024]{2,1,0:T(8,128)} async-done(((f32[2,64,4096]{2,1,0:T(8,128)}), f32[2,64,1024]{2,1,0:T(8,128)}) %reduce-scatter.2.cloned.1.call-update) | async-done | bytes 524304 | tf_op jit(solution)/shard_map/reduce_scatter | solution.py:38
  (48 shorter events, 7.9 us)
Async XLA Ops:
  6.5 126.3 %copy-start.7 = (bf16[3,2,64,4096]{3,2,1,0:T(8,128)(2,1)S(1)}, bf16[3,2,64,4096]{3,2,1,0:T(8,128)(2,1)}, u32[]{:S(2)}) copy-start(bf16[3,2,64,4096]{3,2,1,0:T(8,128)(2,1)} %param.2) | copy-start | bytes 9437188
  6.5 122.7 %all-gather.18.cloned.1.call-start = ((), (), s32[]{:S(2)}) async-start(), calls=%async_computation.6 | async-start | bytes 2129920 | tf_op jit(solution)/shard_map/all_gather | solution.py:22
  8.1 239.4 %all-gather.20.cloned.1.call-start = ((), (), s32[]{:S(2)}) async-start(), calls=%async_computation.7 | async-start | bytes 2129920 | tf_op jit(solution)/shard_map/all_gather | solution.py:22
  8.9 357.0 %all-gather.16.cloned.1.call-start = ((), (), s32[]{:S(2)}) async-start(), calls=%async_computation.5 | async-start | bytes 2129920 | tf_op jit(solution)/shard_map/all_gather | solution.py:22
  9.6 474.4 %all-gather.12.cloned.1.call-start = ((), (), s32[]{:S(2)}) async-start(), calls=%async_computation.2 | async-start | bytes 2129920 | tf_op jit(solution)/shard_map/all_gather | solution.py:34
  130.9 3.4 copy-start.10
  135.3 466.8 %all-gather.14.cloned.1.call-start = ((), (), s32[]{:S(2)}) async-start(), calls=%async_computation.3 | async-start | bytes 2129920 | tf_op jit(solution)/shard_map/all_gather | solution.py:34
  247.5 3.2 copy-start.9
  252.1 468.2 %all-gather.10.cloned.1.call-start = ((), (), s32[]{:S(2)}) async-start(), calls=%async_computation.1 | async-start | bytes 2129920 | tf_op jit(solution)/shard_map/all_gather | solution.py:34
  365.9 3.2 copy-start.8
  370.4 390.5 %reduce-scatter.2.cloned.1.call-start = ((), (), s32[]{:S(2)}) async-start(), calls=%async_computation.4 | async-start | bytes 2621440 | tf_op jit(solution)/shard_map/reduce_scatter | solution.py:38
  484.0 2.8 copy-start
  602.2 2.8 copy-start.1
  720.3 1.9 copy-start.3
  720.3 2.4 copy-start.6
  722.7 1.2 copy-start.4
  723.9 1.6 copy-start.2
  723.9 1.9 copy-start.5
Sparse Core Ops, SparseCore 0:
  10.9 118.3 all-gather.17
  132.7 114.7 all-gather.19
  251.1 114.7 all-gather.15
  369.2 114.7 all-gather.11
  487.4 114.7 all-gather.13
  605.5 114.7 all-gather.9
  729.6 31.2 reduce-scatter.1
where the time goes:
time: 768 us
  waiting for transfers between devices  721 us (94%)
  matrix products  25.9 us (3%)
  between operations  13.7 us (2%)
    all_gather x3, waiting for transfers between devices, on_device(): piece = lax.all_gather(snapshots[index], 'row', axis=1, tiled=True)  345 us
    all_gather x3, waiting for transfers between devices, on_device(): gram_piece = lax.all_gather(current, 'row', axis=1, tiled=True)  342 us
    reduce_scatter x1, waiting for transfers between devices, on_device(): lax.psum_scatter(total * scale, 'bin', scatter_dimension=2, tiled=True)  31.4 us
  transfers between devices with their start and end apart: 7, of which 7 were waited for; matrix products, arithmetic and copies ran while one was open for 3% of the time, Pallas kernels for 0%

commit v1 on v0

--- a/solution.py
+++ b/solution.py
@@ -2,6 +2,7 @@
 import jax.numpy as jnp
 from jax import lax
 from jax.sharding import PartitionSpec as P
+from jax.lax import all_to_all, axis_size
 
 
 def contract(left, right):
@@ -31,7 +32,10 @@
     total = jnp.zeros((2, own_rows, width), jnp.float32)
     for index in range(local_bins):
         current = focused[index]
-        gram_piece = lax.all_gather(current, "row", axis=1, tiled=True)
+        work_now = axis_size("row")
+        all_values = jnp.stack(work_now * [current])
+        value_now = all_to_all(all_values, "row", 0, 0)
+        gram_piece = jnp.concatenate(value_now, 1)
         real_part = contract(current[0], gram_piece[0]) + contract(current[1], gram_piece[1])
         imag_part = contract(current[1], gram_piece[0]) - contract(current[0], gram_piece[1])
         total = total + jnp.stack([real_part, imag_part])

time: 768 us -> 486 us (0.63)
  waiting for transfers between devices: 721 us -> 405 us
  starting transfers between devices: 0.25 us -> 23.7 us
  local copies, waits for them, and re-layouts: 3.76 us -> 12.3 us
    all_gather x3 -> x0, waiting for transfers between devices: 342 us -> none  [on_device(): gram_piece = lax.all_gather(current, 'row', axis=1, tiled=True)]
    all_to_all x0 -> x3, waiting for transfers between devices: none -> 36.8 us  [on_device(): value_now = all_to_all(all_values, 'row', 0, 0)]
    all_to_all x0 -> x3, starting transfers between devices: none -> 23.6 us  [on_device(): value_now = all_to_all(all_values, 'row', 0, 0)]
    all_gather x3, waiting for transfers between devices: 345 us -> 332 us  [on_device(): piece = lax.all_gather(snapshots[index], 'row', axis=1, tiled=True)]
  transfers between devices with their start and end apart: 7 -> 7, of which waited for: 7 -> 5; matrix products, arithmetic and copies ran while one was open for 3% -> 6% of each run, Pallas kernels for 0% -> 0%
where the time goes in v1:
time: 486 us; the launch traced here: 485 us
  waiting for transfers between devices  405 us (83%)
  matrix products  28.5 us (6%)
  starting transfers between devices  23.7 us (5%)
  between operations  13.4 us (3%)
  local copies, waits for them, and re-layouts  12.3 us (3%)
    all_gather x3, waiting for transfers between devices, on_device(): piece = lax.all_gather(snapshots[index], 'row', axis=1, tiled=True)  332 us
    all_to_all x3, waiting for transfers between devices, on_device(): value_now = all_to_all(all_values, 'row', 0, 0)  36.8 us
    reduce_scatter x1, waiting for transfers between devices, on_device(): lax.psum_scatter(total * scale, 'bin', scatter_dimension=2, tiled=True)  34.6 us
    all_to_all x3, starting transfers between devices, on_device(): value_now = all_to_all(all_values, 'row', 0, 0)  23.6 us
    dot_general x12, matrix products, contract(): lax.dot_general(left, right, (((1,), (1,)), ((), ())), preferred_element_...  9.78 us
  transfers between devices with their start and end apart: 7, of which 5 were waited for; matrix products, arithmetic and copies ran while one was open for 6% of the time, Pallas kernels for 0%

profile of v1, /device:TPU:1, one launch (start us, length us, event | category | flops | bytes accessed | tf_op | source)
XLA Modules:
  0.0 484.9 jit_solution(7769427793199661296)
XLA Ops:
  8.7 120.5 %all-gather.11.cloned.1.call-done = bf16[1,2,4096,128]{3,2,1,0:T(8,128)(2,1)} async-done(((bf16[1,2,64,128]{3,2,1,0:T(8,128)(2,1)}), bf16[1,2,4096,128]{3,2,1,0:T(8,128)(2,1)}) %all-gather.11.cloned.1.call-update) | async-done | bytes 2097168 | tf_op jit(solution)/shard_map/all_gather | solution.py:23
  129.2 1.8 fusion.19
  131.1 1.7 fusion.18
  135.5 1.9 stack.92
  137.4 7.7 %all-to-all-start.2 = ((bf16[64,2,64,128]{3,2,1,0:T(8,128)(2,1)}), bf16[64,2,64,128]{3,2,1,0:T(8,128)(2,1)S(1)}, u32[]{:S(2)}, u32[]{:S(2)}) async-start(bf16[64,2,64,128]{3,2,1,0:T(8,128)(2,1)} %stack.92), calls=%async_computation.2 | async-start | bytes 4194304 | tf_op jit(solution)/shard_map/all_to_all | solution.py:37
  145.9 105.5 %all-gather.7.cloned.1.call-done = bf16[1,2,4096,128]{3,2,1,0:T(8,128)(2,1)} async-done(((bf16[1,2,64,128]{3,2,1,0:T(8,128)(2,1)}), bf16[1,2,4096,128]{3,2,1,0:T(8,128)(2,1)}) %all-gather.7.cloned.1.call-update) | async-done | bytes 2097168 | tf_op jit(solution)/shard_map/all_gather | solution.py:23
  251.4 1.8 fusion.15
  253.2 1.7 fusion.14
  257.7 1.9 stack.78
  259.6 7.9 %all-to-all-start = ((bf16[64,2,64,128]{3,2,1,0:T(8,128)(2,1)}), bf16[64,2,64,128]{3,2,1,0:T(8,128)(2,1)}, u32[]{:S(2)}, u32[]{:S(2)}) async-start(bf16[64,2,64,128]{3,2,1,0:T(8,128)(2,1)} %stack.78), calls=%async_computation | async-start | bytes 4194304 | tf_op jit(solution)/shard_map/all_to_all | solution.py:37
  267.5 106.5 %all-gather.9.cloned.1.call-done = bf16[1,2,4096,128]{3,2,1,0:T(8,128)(2,1)} async-done(((bf16[1,2,64,128]{3,2,1,0:T(8,128)(2,1)}), bf16[1,2,4096,128]{3,2,1,0:T(8,128)(2,1)}) %all-gather.9.cloned.1.call-update) | async-done | bytes 2097168 | tf_op jit(solution)/shard_map/all_gather | solution.py:23
  374.0 1.8 fusion.17
  375.8 1.7 fusion.16
  380.3 1.9 stack.85
  382.2 7.9 %all-to-all-start.1 = ((bf16[64,2,64,128]{3,2,1,0:T(8,128)(2,1)}), bf16[64,2,64,128]{3,2,1,0:T(8,128)(2,1)}, u32[]{:S(2)}, u32[]{:S(2)}) async-start(bf16[64,2,64,128]{3,2,1,0:T(8,128)(2,1)} %stack.85), calls=%async_computation.1 | async-start | bytes 4194304 | tf_op jit(solution)/shard_map/all_to_all | solution.py:37
  390.4 1.4 fusion.53
  391.8 1.6 fusion.52
  393.4 1.7 fusion.46
  395.1 1.5 fusion.49
  396.6 1.4 fusion.48
  398.0 36.8 %all-to-all-done.1 = bf16[64,2,64,128]{3,2,1,0:T(8,128)(2,1)} async-done(((bf16[64,2,64,128]{3,2,1,0:T(8,128)(2,1)}), bf16[64,2,64,128]{3,2,1,0:T(8,128)(2,1)}, u32[]{:S(2)}, u32[]{:S(2)}) %all-to-all-start.1) | async-done | bytes 2097184 | tf_op jit(solution)/shard_map/all_to_all | solution.py:37
  434.9 1.7 fusion.45
  442.1 1.7 fusion.7
  443.8 34.6 %reduce-scatter.2.cloned.1.call-done = f32[2,64,1024]{2,1,0:T(8,128)} async-done(((f32[2,64,4096]{2,1,0:T(8,128)}), f32[2,64,1024]{2,1,0:T(8,128)}) %reduce-scatter.2.cloned.1.call-update) | async-done | bytes 524304 | tf_op jit(solution)/shard_map/reduce_scatter | solution.py:42
  (43 shorter events, 16.8 us)
Async XLA Ops:
  6.5 122.7 %all-gather.11.cloned.1.call-start = ((), (), s32[]{:S(2)}) async-start(), calls=%async_computation.7 | async-start | bytes 2129920 | tf_op jit(solution)/shard_map/all_gather | solution.py:23
  8.0 243.4 %all-gather.7.cloned.1.call-start = ((), (), s32[]{:S(2)}) async-start(), calls=%async_computation.5 | async-start | bytes 2129920 | tf_op jit(solution)/shard_map/all_gather | solution.py:23
  129.2 3.6 copy-start.6
  137.4 120.2 %all-to-all-start.2 = ((bf16[64,2,64,128]{3,2,1,0:T(8,128)(2,1)}), bf16[64,2,64,128]{3,2,1,0:T(8,128)(2,1)S(1)}, u32[]{:S(2)}, u32[]{:S(2)}) async-start(bf16[64,2,64,128]{3,2,1,0:T(8,128)(2,1)} %stack.92), calls=%async_computation.2 | async-start | bytes 4194304 | tf_op jit(solution)/shard_map/all_to_all | solution.py:37
  145.1 228.9 %all-gather.9.cloned.1.call-start = ((), (), s32[]{:S(2)}) async-start(), calls=%async_computation.6 | async-start | bytes 2129920 | tf_op jit(solution)/shard_map/all_gather | solution.py:23
  251.4 3.6 copy-start.4
  259.6 120.7 %all-to-all-start = ((bf16[64,2,64,128]{3,2,1,0:T(8,128)(2,1)}), bf16[64,2,64,128]{3,2,1,0:T(8,128)(2,1)}, u32[]{:S(2)}, u32[]{:S(2)}) async-start(bf16[64,2,64,128]{3,2,1,0:T(8,128)(2,1)} %stack.78), calls=%async_computation | async-start | bytes 4194304 | tf_op jit(solution)/shard_map/all_to_all | solution.py:37
  374.0 3.6 copy-start.5
  382.2 52.7 %all-to-all-start.1 = ((bf16[64,2,64,128]{3,2,1,0:T(8,128)(2,1)}), bf16[64,2,64,128]{3,2,1,0:T(8,128)(2,1)}, u32[]{:S(2)}, u32[]{:S(2)}) async-start(bf16[64,2,64,128]{3,2,1,0:T(8,128)(2,1)} %stack.85), calls=%async_computation.1 | async-start | bytes 4194304 | tf_op jit(solution)/shard_map/all_to_all | solution.py:37
  390.1 88.2 %reduce-scatter.2.cloned.1.call-start = ((), (), s32[]{:S(2)}) async-start(), calls=%async_computation.4 | async-start | bytes 2621440 | tf_op jit(solution)/shard_map/reduce_scatter | solution.py:42
  436.6 1.2 copy-start.3
  437.6 1.3 copy-start.1
  438.9 1.2 copy-start.2
  439.4 1.3 copy-start
Sparse Core Ops, SparseCore 0:
  10.9 118.3 all-gather.10
  132.7 118.5 all-gather.6
  254.9 119.0 all-gather.8
  443.9 34.4 reduce-scatter.1
